TPU v7x, 256 devices: a whole 4x4x8 slice. The times are simulated.
256 devices in a mesh: lat: 64 (over x, z, core), fld: 4 (over y).
Axes of the slice: x: 4, y: 4, z: 8, core: 2. Of those that a mesh axis runs over, the one named last changes fastest.
Arguments:
- fourier: bfloat16 [2, 2560, 16, 2, 1280], P(None, 'lat', 'fld'), may hold values from -6 to 6
- legendre: bfloat16 [819840, 1280], P('lat', 'fld'), may hold values from -0.125 to 0.125
- cycle_points: int32 [2560], P('lat'), may hold values from 8 to 5136, as said below
- wave_order: int32 [1280], replicated, may hold values from 0 to 1279, as said below
Outputs:
- spectral: float32 [2, 32, 819840], P(None, 'fld', 'lat')
Inputs may be any that keep to these rules, and one draw needn't show every extreme that they name: `cycle_points`: rows r and r + 1280 hold the same count; for r < 1280 the count is 20 + 4 r minus 0, 4, 8 or 12; row 0 holds 8 and row 1279 holds 5136. `wave_order`: every wavenumber appears once; entries 2 k and 2 k + 1 are a wavenumber below 640 and 1279 minus it.
All inputs are finite; a program needn't handle non-finite values.
Results may differ from a plain program's by a relative error of at most 0.0031.
Values may be sent and summed in bfloat16 or wider, within the bound.
A program may use at most 128 MiB of HBM per device.

v0:
```python
import functools

import jax
import jax.numpy as jnp
from jax import lax
from jax.experimental import pallas as pl
from jax.experimental.pallas import tpu as pltpu
from jax.sharding import PartitionSpec as P

MESH = pl.DeviceIdType.MESH
NT = (((1,), (1,)), ((), ()))
ROW_PAD = 24


def round_up(value, step):
    return -(-value // step) * step


def exchange_kernel(
    n_lat,
    n_fld,
    lane_tile,
    x_ref,
    waves_ref,
    limit_ref,
    owned_ref,
    legendre_ref,
    out_ref,
    send_buf,
    recv_buf,
    tables,
    mixed_sym,
    mixed_anti,
    rows_sym,
    rows_anti,
    partial,
    part_send,
    part_recv,
    send_sem,
    recv_sem,
    table_sem,
    part_send_sem,
    part_recv_sem,
):
    lat = lax.axis_index("lat")
    fld = lax.axis_index("fld")
    half = n_lat // 2
    depth = half // n_fld
    hemi = lat // half
    block = (lat % half) // depth
    place = lat % depth
    owner_waves, columns = send_buf.shape[1], send_buf.shape[2]
    wave_count = x_ref.shape[1]
    kinds = part_send.shape[1]
    rows_each = columns // kinds
    pairs = owner_waves // 2
    own = block == fld
    lat_depth, total = legendre_ref.shape

    load = pltpu.make_async_copy(legendre_ref, tables, table_sem)
    load.start()

    barrier = pltpu.get_barrier_semaphore()

    def greet(s, carry):
        source_fld = s // (2 * depth)
        rest = s % (2 * depth)
        source_lat = (rest // depth) * half + fld * depth + rest % depth
        itself = jnp.logical_and(source_lat == lat, source_fld == fld)

        @pl.when(jnp.logical_not(itself))
        def _():
            pl.semaphore_signal(
                barrier, inc=1, device_id=(source_lat, source_fld), device_id_type=MESH
            )

        return carry

    lax.fori_loop(0, n_fld * 2 * depth, greet, 0)
    for d in range(1, n_fld):
        pl.semaphore_signal(
            barrier, inc=1, device_id=(lat, (fld + d) % n_fld), device_id_type=MESH
        )

    slot = (fld * 2 + hemi) * depth + place

    def copy_to(owner):
        return pltpu.make_async_remote_copy(
            src_ref=send_buf.at[owner],
            dst_ref=recv_buf.at[slot],
            send_sem=send_sem.at[owner],
            recv_sem=recv_sem.at[slot],
            device_id=(owner, block),
            device_id_type=MESH,
        )

    group = min(8, n_lat)
    groups = n_lat // group
    lane = lax.broadcasted_iota(jnp.int32, (group * ROW_PAD, 128), 1)

    def reorder(step):
        number = (lat // group + step) % groups
        start = pl.multiple_of(number * (group * ROW_PAD), group * ROW_PAD)
        wave = waves_ref[pl.ds(start, group * ROW_PAD), :]
        pieces = []
        for v in range(-(-wave_count // 128)):
            width = min(128, wave_count - 128 * v)
            hit = jnp.where(wave == lane + 128 * v, 1.0, 0.0).astype(jnp.bfloat16)
            pieces.append(hit[:, :width])
        chosen = jnp.concatenate(pieces, axis=1)
        picked = lax.dot_general(
            chosen, x_ref[...], NT, preferred_element_type=jnp.float32
        )
        wide = jnp.concatenate([wave] * (-(-columns // 128)), axis=1)[:, :columns]
        picked = jnp.where(wide < limit_ref[...], picked, 0.0)
        for o in range(group):
            part = picked[o * ROW_PAD : o * ROW_PAD + owner_waves]
            send_buf[number * group + o] = part.astype(jnp.bfloat16)
        return number

    def send(number):
        def one(o, carry):
            owner = number * group + (lat + o) % group
            itself = jnp.logical_and(own, owner == lat)

            @pl.when(itself)
            def _():
                pltpu.make_async_copy(
                    send_buf.at[owner], recv_buf.at[slot], recv_sem.at[slot]
                ).start()

            @pl.when(jnp.logical_not(itself))
            def _():
                copy_to(owner).start()

            return carry

        lax.fori_loop(0, group, one, 0)

    number = reorder(0)
    pl.semaphore_wait(barrier, n_lat + n_fld - 1 - own.astype(jnp.int32))
    send(number)

    def sender(step, carry):
        send(reorder(step))
        return carry

    lax.fori_loop(1, groups, sender, 0)
    load.wait()

    def arrived(s, carry):
        pltpu.make_async_copy(recv_buf.at[s], recv_buf.at[s], recv_sem.at[s]).wait()
        return carry

    lax.fori_loop(0, n_fld * 2 * depth, arrived, 0)

    def gather_field(f, carry):
        for a in range(depth):
            north = recv_buf[(2 * f) * depth + a].astype(jnp.float32)
            south = recv_buf[(2 * f + 1) * depth + a].astype(jnp.float32)
            mixed_sym[a] = north + south
            mixed_anti[a] = north - south
        for mixed, rows in ((mixed_sym, rows_sym), (mixed_anti, rows_anti)):
            for k in range(kinds):
                lo = k * rows_each
                joined = jnp.concatenate(
                    [mixed[a, :, lo : lo + rows_each] for a in range(depth)], axis=1
                )
                for v in range(-(-lat_depth // 128)):
                    width = min(128, lat_depth - 128 * v)
                    rows[
                        v,
                        pl.ds(f * kinds + k, owner_waves, stride=n_fld * kinds),
                        0:width,
                    ] = joined[:, 128 * v : 128 * v + width]
        return carry

    lax.fori_loop(0, n_fld, gather_field, 0)

    per_wave = n_fld * kinds
    even = wave_count // 2 + 1
    sym_end = round_up(even + pairs, lane_tile)
    anti_start = even // lane_tile * lane_tile

    def operand(rows, pair):
        start = pl.multiple_of(pair * (2 * per_wave), 2 * per_wave)
        parts = []
        for v in range(-(-lat_depth // 128)):
            width = min(128, lat_depth - 128 * v)
            parts.append(rows[v, pl.ds(start, 2 * per_wave), 0:width])
        return jnp.concatenate(parts, axis=1).astype(jnp.bfloat16)

    def project(left, start, width):
        return jnp.dot(left, tables[:, pl.ds(start, width)], preferred_element_type=jnp.float32)

    def choose(product, first):
        return jnp.where(first, product[:per_wave], product[per_wave:])

    def degree_index(width, offset):
        return lax.broadcasted_iota(jnp.int32, (per_wave, width), 1) + offset

    def part_copy(d, lo, width, number):
        peer = (fld + d) % n_fld
        return pltpu.make_async_remote_copy(
            src_ref=part_send.at[peer, :, pl.ds(lo, width)],
            dst_ref=part_recv.at[d - 1, :, pl.ds(lo, width)],
            send_sem=part_send_sem.at[d - 1, number],
            recv_sem=part_recv_sem.at[d - 1, number],
            device_id=(lat, peer),
            device_id_type=MESH,
        )

    def left_over(pair, start, width):
        first_rows = lax.shift_right_logical(wave_count - owned_ref[2 * pair], 1)
        product = project(operand(rows_anti, pair), start, width)
        degree = degree_index(width, 0) + (wave_count // 2 - 1 - pair)
        return choose(product, degree < first_rows)

    def pair_chunk(c, carry):
        start = pl.multiple_of(c * wave_count, min(wave_count, 1280))
        wave = owned_ref[2 * c]
        first_even = lax.shift_right_logical(wave_count + 1 - wave, 1)
        first_odd = lax.shift_right_logical(wave_count - wave, 1)
        sym = project(operand(rows_sym, c), start, sym_end)
        sym = choose(sym, degree_index(sym_end, -c) < first_even)
        anti_width = wave_count - anti_start
        anti_from = pl.multiple_of(start + anti_start, lane_tile)
        anti = project(operand(rows_anti, c), anti_from, anti_width)
        anti = choose(anti, degree_index(anti_width, anti_start - even - c) < first_odd)
        before = left_over(jnp.maximum(c - 1, 0), start, lane_tile)
        head = jnp.where(degree_index(lane_tile, 0) < c, before, sym[:, :lane_tile])
        middle = jnp.where(
            degree_index(sym_end - anti_start, anti_start - c) < even,
            sym[:, anti_start:],
            anti[:, : sym_end - anti_start],
        )
        pieces = [head, sym[:, lane_tile:anti_start], middle, anti[:, sym_end - anti_start :]]
        at = 0
        for piece in pieces:
            width = piece.shape[1]
            if width == 0:
                continue
            lanes = pl.ds(pl.multiple_of(start + at, lane_tile), width)
            partial[:, lanes] = piece
            for f in range(n_fld):
                part_send[f, :, lanes] = piece[f * kinds : (f + 1) * kinds].astype(jnp.bfloat16)
            at += width
        for d in range(1, n_fld):
            part_copy(d, start, wave_count, c).start()
        return carry

    lax.fori_loop(0, pairs, pair_chunk, 0)

    tail = total - pairs * wave_count
    tail_from = pairs * wave_count
    piece = left_over(pairs - 1, tail_from, tail)
    partial[:, tail_from : tail_from + tail] = piece
    for f in range(n_fld):
        part_send[f, :, tail_from : tail_from + tail] = piece[
            f * kinds : (f + 1) * kinds
        ].astype(jnp.bfloat16)
    tail_wide = part_send.shape[2] - tail_from
    for d in range(1, n_fld):
        part_copy(d, tail_from, tail_wide, pairs).start()

    mine = pl.multiple_of(fld * kinds, kinds)
    batch_rows = kinds // 2

    def finish(lo, width, kept, number):
        for d in range(1, n_fld):
            part_copy(d, lo, width, number).wait_recv()
        result = partial[pl.ds(mine, kinds), pl.ds(lo, kept)]
        for d in range(1, n_fld):
            result = result + part_recv[d - 1, :, pl.ds(lo, kept)].astype(jnp.float32)
        out_ref[0, :, pl.ds(lo, kept)] = result[:batch_rows]
        out_ref[1, :, pl.ds(lo, kept)] = result[batch_rows:]

    def finish_pair(c, carry):
        start = pl.multiple_of(c * wave_count, min(wave_count, 1280))
        finish(start, wave_count, wave_count, c)
        return carry

    lax.fori_loop(0, pairs, finish_pair, 0)
    finish(tail_from, tail_wide, tail, pairs)

    def sent(owner, carry):
        @pl.when(jnp.logical_not(jnp.logical_and(own, owner == lat)))
        def _():
            copy_to(owner).wait_send()

        return carry

    lax.fori_loop(0, n_lat, sent, 0)

    def part_sent(c, carry):
        start = pl.multiple_of(c * wave_count, min(wave_count, 1280))
        for d in range(1, n_fld):
            part_copy(d, start, wave_count, c).wait_send()
        return carry

    lax.fori_loop(0, pairs, part_sent, 0)
    for d in range(1, n_fld):
        part_copy(d, tail_from, tail_wide, pairs).wait_send()


def shards(fourier, legendre, cycle_points, wave_order, lane_tile=256):
    n_lat, n_fld = lax.axis_size("lat"), lax.axis_size("fld")
    batches, rows_each, fields, parts, wave_count = fourier.shape
    kinds = batches * fields * parts
    columns = kinds * rows_each
    owner_waves = wave_count // n_lat
    total, lat_depth = legendre.shape
    depth = n_lat // 2 // n_fld
    per_wave = n_fld * kinds
    padded = round_up(total, 128)
    tiles = -(-lat_depth // 128)

    x = jnp.transpose(fourier, (0, 2, 3, 1, 4)).reshape(columns, wave_count)
    waves = jnp.pad(
        wave_order.reshape(n_lat, owner_waves),
        ((0, 0), (0, ROW_PAD - owner_waves)),
        constant_values=-1,
    ).reshape(n_lat * ROW_PAD, 1)
    waves = jnp.broadcast_to(waves, (n_lat * ROW_PAD, 128))
    limit = jnp.tile(jnp.minimum(cycle_points // 2, wave_count), kinds).reshape(1, columns)
    owned = lax.dynamic_slice_in_dim(
        wave_order, lax.axis_index("lat") * owner_waves, owner_waves
    )
    vmem = pl.BlockSpec(memory_space=pltpu.VMEM)
    return pl.pallas_call(
        functools.partial(exchange_kernel, n_lat, n_fld, lane_tile),
        out_shape=jax.ShapeDtypeStruct((batches, fields * parts, total), jnp.float32),
        in_specs=[
            vmem,
            vmem,
            vmem,
            pl.BlockSpec(memory_space=pltpu.SMEM),
            pl.BlockSpec(memory_space=pl.ANY),
        ],
        out_specs=vmem,
        scratch_shapes=[
            pltpu.VMEM((n_lat, owner_waves, columns), jnp.bfloat16),
            pltpu.VMEM((2 * depth * n_fld, owner_waves, columns), jnp.bfloat16),
            pltpu.VMEM((lat_depth, total), jnp.bfloat16),
            pltpu.VMEM((depth, owner_waves, columns), jnp.float32),
            pltpu.VMEM((depth, owner_waves, columns), jnp.float32),
            pltpu.VMEM((tiles, owner_waves * per_wave, 128), jnp.float32),
            pltpu.VMEM((tiles, owner_waves * per_wave, 128), jnp.float32),
            pltpu.VMEM((per_wave, padded), jnp.float32),
            pltpu.VMEM((n_fld, kinds, padded), jnp.bfloat16),
            pltpu.VMEM((n_fld - 1, kinds, padded), jnp.bfloat16),
            pltpu.SemaphoreType.DMA((n_lat,)),
            pltpu.SemaphoreType.DMA((2 * depth * n_fld,)),
            pltpu.SemaphoreType.DMA,
            pltpu.SemaphoreType.DMA((n_fld - 1, owner_waves // 2 + 1)),
            pltpu.SemaphoreType.DMA((n_fld - 1, owner_waves // 2 + 1)),
        ],
        compiler_params=pltpu.CompilerParams(
            collective_id=0, has_side_effects=True, vmem_limit_bytes=56 * 2**20
        ),
        cost_estimate=pl.CostEstimate(
            flops=4 * columns * wave_count * wave_count,
            bytes_accessed=total * lat_depth * 2,
            transcendentals=0,
        ),
    )(x, waves, limit, owned, legendre.T)


def solution(mesh):
    placed = (P(None, "lat", "fld", None, None), P("lat", "fld"), P("lat"), P())
    return jax.shard_map(
        shards, mesh=mesh, in_specs=placed, out_specs=P(None, "fld", "lat"), check_vma=False
    )
```

profile of v0, /device:TPU:1, one launch (start us, length us, event | category | flops | bytes accessed | tf_op | source)
XLA Modules:
  0.0 100.6 jit_solution(9482293315897640489)
XLA Ops:
  0.0 1.3 %dynamic_slice.3.owned_ref = s32[20]{0:T(128)} dynamic-slice(s32[1280]{0:T(1024)} %param.7, s32[]{:T(128)S(6)} %select_n.9), dynamic_slice_sizes={20} | dynamic-slice | bytes 164 | tf_op jit(solution)/shard_map/dynamic_slice | solution.py:326
  1.3 0.7 fusion
  2.0 0.7 reshape_tile.3.limit_ref
  2.7 0.8 reshape.10
  3.5 0.1 broadcast_in_dim.7
  3.6 1.1 %broadcast_in_dim.8.waves_ref = s32[1536,128]{1,0:T(8,128)} broadcast(s32[1536]{0:T(1024)S(1)} %broadcast_in_dim.7), dimensions={0} | broadcast | bytes 792576 | tf_op jit(solution)/shard_map/broadcast_in_dim | solution.py:324
  4.7 2.9 %copy.6 = bf16[2,4,2,40,1280]{4,3,2,1,0:T(8,128)(2,1)} copy(bf16[2,4,2,40,1280]{4,2,1,3,0:T(2,128)(2,1)} %bitcast.3) | data formatting | bytes 3276800 | tf_op jit(solution)/shard_map/transpose | solution.py:318
  7.6 90.9 %shard_map.46 = f32[2,8,12810]{2,1,0:T(8,128)} custom-call(bf16[640,1280]{1,0:T(8,128)(2,1)} %bitcast.4, s32[1536,128]{1,0:T(8,128)} %broadcast_in_dim.8.waves_ref, s32[1,640]{1,0:T(1,128)} %reshape_tile.3.limit_ref, s32[20]{0:T(128)} %dynamic_slice.3.owned_ref, bf16[320,12810]{1,0:T(8,128)(2,1)} %bitcast.5), custom_call_target="tpu_custom_call" | custom-call | flops 4194304000 | bytes 8198400 | tf_op jit(solution)/shard_map/pallas_call | solution.py:330
  98.5 2.1 %copy.8 = f32[2,8,12810]{2,1,0:T(8,128)} copy(f32[2,8,12810]{2,1,0:T(8,128)} %shard_map.46) | data formatting | bytes 1639680
  (2 shorter events, 0.0 us)
where the time goes:
time: 101 us
  Pallas kernels  90.9 us (90%)
  local copies, waits for them, and re-layouts  9.01 us (9%)
    pallas_call x1, Pallas kernels, shards(): pl.pallas_call(functools.partial(exchange_kernel, n_lat, n_fld, lane_tile...  90.9 us
    transpose x1, local copies, waits for them, and re-layouts, shards(): x = jnp.transpose(fourier, (0, 2, 3, 1, 4)).reshape(columns, wave_count)  2.9 us
    unnamed x1, local copies, waits for them, and re-layouts  2.09 us

commit v1 on v0

v1 whole, which is shorter than its diff:
```python
import functools

import jax
import jax.numpy as jnp
from jax import lax
from jax.experimental import pallas as pl
from jax.experimental.pallas import tpu as pltpu
from jax.sharding import PartitionSpec as P

MESH = pl.DeviceIdType.MESH
NT = (((1,), (1,)), ((), ()))


def round_up(value, step):
    return -(-value // step) * step


def exchange_kernel(
    n_lat,
    n_fld,
    lane_tile,
    sizes,
    x_ref,
    waves_ref,
    owned_ref,
    legendre_ref,
    out_ref,
    *scratch,
):
    n_groups = len(sizes)
    send_bufs, scratch = scratch[:n_groups], scratch[n_groups:]
    recv_bufs, scratch = scratch[:n_groups], scratch[n_groups:]
    (
        wave_cols,
        tables,
        mixed_sym,
        mixed_anti,
        rows_sym,
        rows_anti,
        partial,
        part_send,
        part_recv,
        send_sem,
        recv_sem,
        table_sem,
        part_send_sem,
        part_recv_sem,
    ) = scratch
    lat = lax.axis_index("lat")
    fld = lax.axis_index("fld")
    half = n_lat // 2
    depth = half // n_fld
    sources = 2 * depth
    hemi = lat // half
    block = (lat % half) // depth
    place = lat % depth
    columns, wave_count = x_ref.shape
    owner_waves = sum(sizes)
    kinds = part_send.shape[1]
    rows_each = columns // kinds
    pairs = owner_waves // 2
    own = block == fld
    lat_depth, total = legendre_ref.shape
    first_owned = lat * owner_waves

    load = pltpu.make_async_copy(legendre_ref, tables, table_sem)
    load.start()

    barrier = pltpu.get_barrier_semaphore()

    def greet(s, carry):
        source_fld = s // sources
        rest = s % sources
        source_lat = (rest // depth) * half + fld * depth + rest % depth
        itself = jnp.logical_and(source_lat == lat, source_fld == fld)

        @pl.when(jnp.logical_not(itself))
        def _():
            pl.semaphore_signal(
                barrier, inc=1, device_id=(source_lat, source_fld), device_id_type=MESH
            )

        return carry

    lax.fori_loop(0, n_fld * sources, greet, 0)
    for d in range(1, n_fld):
        pl.semaphore_signal(
            barrier, inc=1, device_id=(lat, (fld + d) % n_fld), device_id_type=MESH
        )

    slot = fld * sources + hemi * depth + place

    def copy_to(number, owner):
        return pltpu.make_async_remote_copy(
            src_ref=send_bufs[number].at[owner],
            dst_ref=recv_bufs[number].at[slot],
            send_sem=send_sem.at[number, owner],
            recv_sem=recv_sem.at[number, slot],
            device_id=(owner, block),
            device_id_type=MESH,
        )

    for v in range(-(-wave_count // 128)):
        width = min(128, wave_count - 128 * v)
        line = waves_ref[:, 128 * v : 128 * v + width]
        wave_cols[128 * v : 128 * v + width] = jnp.broadcast_to(line, (128, width)).T

    wave_cols[wave_count : wave_count + 8] = jnp.full((8, 128), -1, jnp.int32)

    lane = lax.broadcasted_iota(jnp.int32, (n_lat * 8, 128), 1)

    def reorder(number):
        first = 8 * number
        wave = jnp.concatenate(
            [wave_cols[o * owner_waves + first : o * owner_waves + first + 8] for o in range(n_lat)],
            axis=0,
        )
        pieces = []
        for v in range(-(-wave_count // 128)):
            width = min(128, wave_count - 128 * v)
            hit = jnp.where(wave == lane + 128 * v, 1.0, 0.0).astype(jnp.bfloat16)
            pieces.append(hit[:, :width])
        chosen = jnp.concatenate(pieces, axis=1)
        picked = lax.dot_general(
            chosen, x_ref[...], NT, preferred_element_type=jnp.float32
        )
        for o in range(n_lat):
            part = picked[8 * o : 8 * o + sizes[number]]
            send_bufs[number][o] = part.astype(jnp.bfloat16)

    def send(number):
        def several(u, carry):
            for n in range(8):
                if n_lat == 64:
                    owner = (
                        (lat // 16 + u % 4 + n) % 4 * 16
                        + (lat // 2 % 8 + (4, 1, 7, 2, 6, 3, 5, 0)[n]) % 8 * 2
                        + (lat + u // 4 + n) % 2
                    )
                else:
                    owner = (lat + u * 8 + n) % n_lat
                itself = jnp.logical_and(own, owner == lat)

                @pl.when(itself)
                def _():
                    pltpu.make_async_copy(
                        send_bufs[number].at[owner],
                        recv_bufs[number].at[slot],
                        recv_sem.at[number, slot],
                    ).start()

                @pl.when(jnp.logical_not(itself))
                def _():
                    copy_to(number, owner).start()

            return carry

        lax.fori_loop(0, n_lat // 8, several, 0)

    for number in range(n_groups):
        reorder(number)
        if number == 0:
            pl.semaphore_wait(barrier, n_lat + n_fld - 1 - own.astype(jnp.int32))
        send(number)

    def gather_group(number):
        count = sizes[number]
        recv_buf = recv_bufs[number]

        def gather_field(f, carry):
            def arrived(s, carry):
                at = f * sources + s
                pltpu.make_async_copy(
                    recv_buf.at[at], recv_buf.at[at], recv_sem.at[number, at]
                ).wait()
                return carry

            lax.fori_loop(0, sources, arrived, 0)
            for a in range(depth):
                north = recv_buf[f * sources + a].astype(jnp.float32)
                south = recv_buf[f * sources + depth + a].astype(jnp.float32)
                mixed_sym[a, 0:count] = north + south
                mixed_anti[a, 0:count] = north - south
            for mixed, rows in ((mixed_sym, rows_sym), (mixed_anti, rows_anti)):
                for k in range(kinds):
                    lo = k * rows_each
                    joined = jnp.concatenate(
                        [mixed[a, 0:count, lo : lo + rows_each] for a in range(depth)], axis=1
                    )
                    start = 8 * number * n_fld * kinds + f * kinds + k
                    for v in range(-(-lat_depth // 128)):
                        width = min(128, lat_depth - 128 * v)
                        rows[v, pl.ds(start, count, stride=n_fld * kinds), 0:width] = joined[
                            :, 128 * v : 128 * v + width
                        ]
            return carry

        lax.fori_loop(0, n_fld, gather_field, 0)

    per_wave = n_fld * kinds
    even = wave_count // 2 + 1
    sym_end = round_up(even + pairs, lane_tile)
    anti_start = even // lane_tile * lane_tile

    def operand(rows, pair):
        start = pl.multiple_of(pair * (2 * per_wave), 2 * per_wave)
        parts = []
        for v in range(-(-lat_depth // 128)):
            width = min(128, lat_depth - 128 * v)
            parts.append(rows[v, pl.ds(start, 2 * per_wave), 0:width])
        return jnp.concatenate(parts, axis=1).astype(jnp.bfloat16)

    def project(left, start, width):
        return jnp.dot(left, tables[:, pl.ds(start, width)], preferred_element_type=jnp.float32)

    def choose(product, first):
        return jnp.where(first, product[:per_wave], product[per_wave:])

    def degree_index(width, offset):
        return lax.broadcasted_iota(jnp.int32, (per_wave, width), 1) + offset

    def part_copy(d, lo, width, number):
        peer = (fld + d) % n_fld
        return pltpu.make_async_remote_copy(
            src_ref=part_send.at[peer, :, pl.ds(lo, width)],
            dst_ref=part_recv.at[d - 1, :, pl.ds(lo, width)],
            send_sem=part_send_sem.at[d - 1, number],
            recv_sem=part_recv_sem.at[d - 1, number],
            device_id=(lat, peer),
            device_id_type=MESH,
        )

    def left_over(pair, start, width):
        first_rows = lax.shift_right_logical(wave_count - owned_ref[first_owned + 2 * pair], 1)
        product = project(operand(rows_anti, pair), start, width)
        degree = degree_index(width, 0) + (wave_count // 2 - 1 - pair)
        return choose(product, degree < first_rows)

    def pair_chunk(c, carry):
        start = pl.multiple_of(c * wave_count, min(wave_count, 1280))
        wave = owned_ref[first_owned + 2 * c]
        first_even = lax.shift_right_logical(wave_count + 1 - wave, 1)
        first_odd = lax.shift_right_logical(wave_count - wave, 1)
        sym = project(operand(rows_sym, c), start, sym_end)
        sym = choose(sym, degree_index(sym_end, -c) < first_even)
        anti_width = wave_count - anti_start
        anti_from = pl.multiple_of(start + anti_start, lane_tile)
        anti = project(operand(rows_anti, c), anti_from, anti_width)
        anti = choose(anti, degree_index(anti_width, anti_start - even - c) < first_odd)
        before = left_over(jnp.maximum(c - 1, 0), start, lane_tile)
        head = jnp.where(degree_index(lane_tile, 0) < c, before, sym[:, :lane_tile])
        middle = jnp.where(
            degree_index(sym_end - anti_start, anti_start - c) < even,
            sym[:, anti_start:],
            anti[:, : sym_end - anti_start],
        )
        pieces = [head, sym[:, lane_tile:anti_start], middle, anti[:, sym_end - anti_start :]]
        at = 0
        for piece in pieces:
            width = piece.shape[1]
            if width == 0:
                continue
            lanes = pl.ds(pl.multiple_of(start + at, lane_tile), width)
            partial[:, lanes] = piece
            for f in range(n_fld):
                part_send[f, :, lanes] = piece[f * kinds : (f + 1) * kinds].astype(jnp.bfloat16)
            at += width
        for d in range(1, n_fld):
            part_copy(d, start, wave_count, c).start()
        return carry

    tail = total - pairs * wave_count
    tail_from = pairs * wave_count
    tail_wide = part_send.shape[2] - tail_from

    mine = pl.multiple_of(fld * kinds, kinds)
    batch_rows = kinds // 2

    def finish(lo, width, kept, number):
        for d in range(1, n_fld):
            part_copy(d, lo, width, number).wait_recv()
        result = partial[pl.ds(mine, kinds), pl.ds(lo, kept)]
        for d in range(1, n_fld):
            result = result + part_recv[d - 1, :, pl.ds(lo, kept)].astype(jnp.float32)
        out_ref[0, :, pl.ds(lo, kept)] = result[:batch_rows]
        out_ref[1, :, pl.ds(lo, kept)] = result[batch_rows:]

    def finish_pair(c, carry):
        start = pl.multiple_of(c * wave_count, min(wave_count, 1280))
        finish(start, wave_count, wave_count, c)
        return carry

    load.wait()
    finished = 0
    for number in range(n_groups):
        gather_group(number)
        first = 4 * number
        lax.fori_loop(first, first + sizes[number] // 2, pair_chunk, 0)
        if number == n_groups - 2:
            finished = 4 * number
            lax.fori_loop(0, finished, finish_pair, 0)

    piece = left_over(pairs - 1, tail_from, tail)
    partial[:, tail_from : tail_from + tail] = piece
    for f in range(n_fld):
        part_send[f, :, tail_from : tail_from + tail] = piece[
            f * kinds : (f + 1) * kinds
        ].astype(jnp.bfloat16)
    for d in range(1, n_fld):
        part_copy(d, tail_from, tail_wide, pairs).start()

    lax.fori_loop(finished, pairs, finish_pair, 0)
    finish(tail_from, tail_wide, tail, pairs)

    for number in range(n_groups):

        def sent(owner, carry):
            @pl.when(jnp.logical_not(jnp.logical_and(own, owner == lat)))
            def _():
                copy_to(number, owner).wait_send()

            return carry

        lax.fori_loop(0, n_lat, sent, 0)

    def part_sent(c, carry):
        start = pl.multiple_of(c * wave_count, min(wave_count, 1280))
        for d in range(1, n_fld):
            part_copy(d, start, wave_count, c).wait_send()
        return carry

    lax.fori_loop(0, pairs, part_sent, 0)
    for d in range(1, n_fld):
        part_copy(d, tail_from, tail_wide, pairs).wait_send()


def shards(fourier, legendre, cycle_points, wave_order, lane_tile=256):
    n_lat, n_fld = lax.axis_size("lat"), lax.axis_size("fld")
    batches, rows_each, fields, parts, wave_count = fourier.shape
    kinds = batches * fields * parts
    columns = kinds * rows_each
    owner_waves = wave_count // n_lat
    total, lat_depth = legendre.shape
    depth = n_lat // 2 // n_fld
    slots = 2 * depth * n_fld
    per_wave = n_fld * kinds
    padded = round_up(total, 128)
    tiles = -(-lat_depth // 128)

    sizes = tuple(min(8, owner_waves - t) for t in range(0, owner_waves, 8))
    wave_limit = jnp.minimum(cycle_points // 2, wave_count)
    keep_mask = jnp.arange(wave_count, dtype=jnp.int32)[None, :] < wave_limit[:, None]
    kept = jnp.where(keep_mask[None, :, None, None, :], fourier, jnp.zeros((), fourier.dtype))
    x = jnp.transpose(kept, (0, 2, 3, 1, 4)).reshape(columns, wave_count)
    vmem = pl.BlockSpec(memory_space=pltpu.VMEM)
    return pl.pallas_call(
        functools.partial(exchange_kernel, n_lat, n_fld, lane_tile, sizes),
        out_shape=jax.ShapeDtypeStruct((batches, fields * parts, total), jnp.float32),
        in_specs=[
            vmem,
            vmem,
            pl.BlockSpec(memory_space=pltpu.SMEM),
            pl.BlockSpec(memory_space=pl.ANY),
        ],
        out_specs=vmem,
        scratch_shapes=[
            *(pltpu.VMEM((n_lat, count, columns), jnp.bfloat16) for count in sizes),
            *(pltpu.VMEM((slots, count, columns), jnp.bfloat16) for count in sizes),
            pltpu.VMEM((round_up(wave_count, 128) + 8, 128), jnp.int32),
            pltpu.VMEM((lat_depth, total), jnp.bfloat16),
            pltpu.VMEM((depth, 8, columns), jnp.float32),
            pltpu.VMEM((depth, 8, columns), jnp.float32),
            pltpu.VMEM((tiles, owner_waves * per_wave, 128), jnp.float32),
            pltpu.VMEM((tiles, owner_waves * per_wave, 128), jnp.float32),
            pltpu.VMEM((per_wave, padded), jnp.float32),
            pltpu.VMEM((n_fld, kinds, padded), jnp.bfloat16),
            pltpu.VMEM((n_fld - 1, kinds, padded), jnp.bfloat16),
            pltpu.SemaphoreType.DMA((len(sizes), n_lat)),
            pltpu.SemaphoreType.DMA((len(sizes), slots)),
            pltpu.SemaphoreType.DMA,
            pltpu.SemaphoreType.DMA((n_fld - 1, owner_waves // 2 + 1)),
            pltpu.SemaphoreType.DMA((n_fld - 1, owner_waves // 2 + 1)),
        ],
        compiler_params=pltpu.CompilerParams(
            collective_id=0, has_side_effects=True, vmem_limit_bytes=56 * 2**20
        ),
        cost_estimate=pl.CostEstimate(
            flops=4 * columns * wave_count * wave_count,
            bytes_accessed=total * lat_depth * 2,
            transcendentals=0,
        ),
    )(x, wave_order.reshape(1, wave_count), wave_order, legendre.T)


def solution(mesh):
    placed = (P(None, "lat", "fld", None, None), P("lat", "fld"), P("lat"), P())
    return jax.shard_map(
        shards, mesh=mesh, in_specs=placed, out_specs=P(None, "fld", "lat"), check_vma=False
    )
```

time: 101 us -> 78.6 us (0.78)
  Pallas kernels: 90.9 us -> 70.4 us
  local copies, waits for them, and re-layouts: 9.01 us -> 4.16 us
  other arithmetic: 0.66 us -> 3.8 us
    pallas_call x1, Pallas kernels: 90.9 us -> 70.4 us  [shards(): pl.pallas_call(functools.partial(exchange_kernel, n_lat, n_fld, lane_tile...]
    transpose x0 -> x1, other arithmetic: none -> 3.03 us  [shards(): x = jnp.transpose(kept, (0, 2, 3, 1, 4)).reshape(columns, wave_count)]
    transpose x1, local copies, waits for them, and re-layouts: 2.9 us -> 1.47 us  [shards(): x = jnp.transpose(kept, (0, 2, 3, 1, 4)).reshape(columns, wave_count)]
    dynamic_slice x1 -> x0, local copies, waits for them, and re-layouts: 1.33 us -> none  [shards(): lax.dynamic_slice_in_dim(wave_order, lax.axis_index('lat') * owner_waves,...]
    broadcast_in_dim x2 -> x0, local copies, waits for them, and re-layouts: 1.23 us -> none  [shards(): waves = jnp.broadcast_to(waves, (n_lat * ROW_PAD, 128))]
    unnamed x1 -> x3, local copies, waits for them, and re-layouts: 2.09 us -> 2.1 us
where the time goes in v1:
time: 78.6 us; the launch traced here: 78.4 us
  Pallas kernels  70.4 us (90%)
  local copies, waits for them, and re-layouts  4.16 us (5%)
  other arithmetic  3.8 us (5%)
    pallas_call x1, Pallas kernels, shards(): pl.pallas_call(functools.partial(exchange_kernel, n_lat, n_fld, lane_tile...  70.4 us
    transpose x1, other arithmetic, shards(): x = jnp.transpose(kept, (0, 2, 3, 1, 4)).reshape(columns, wave_count)  3.03 us
    unnamed x3, local copies, waits for them, and re-layouts  2.1 us

profile of v1, /device:TPU:1, one launch (start us, length us, event | category | flops | bytes accessed | tf_op | source)
XLA Modules:
  0.0 78.4 jit_solution(3117863212722733798)
XLA Ops:
  0.0 0.7 fusion.1
  0.7 0.1 iota_compare_fusion
  0.8 3.0 %fusion = bf16[2,4,2,40,1280]{4,2,1,3,0:T(2,128)(2,1)S(1)} fusion(bf16[2,40,4,2,1280]{4,3,2,1,0:T(2,128)(2,1)} %param.4, pred[40,1280]{1,0:T(8,128)(4,1)S(1)} %iota_compare_fusion), kind=kLoop, calls=%fused_computation.1 | loop fusion | flops 819200 | bytes 3328000 | tf_op jit(solution)/shard_map/transpose | solution.py:354
  3.8 0.0 copy-start
  3.8 1.5 %copy.5 = bf16[2,4,2,40,1280]{4,3,2,1,0:T(8,128)(2,1)} copy(bf16[2,4,2,40,1280]{4,2,1,3,0:T(2,128)(2,1)S(1)} %fusion) | data formatting | bytes 3276800 | tf_op jit(solution)/shard_map/transpose | solution.py:354
  5.3 0.0 copy-done
  5.3 0.6 reshape.25.waves_ref
  5.9 70.4 %shard_map.46 = f32[2,8,12810]{2,1,0:T(8,128)} custom-call(bf16[640,1280]{1,0:T(8,128)(2,1)} %bitcast.4, s32[1,1280]{1,0:T(1,128)} %reshape.25.waves_ref, s32[1280]{0:T(1024)} %owned_ref.1, bf16[320,12810]{1,0:T(8,128)(2,1)} %bitcast.5), custom_call_target="tpu_custom_call" | custom-call | flops 4194304000 | bytes 8198400 | tf_op jit(solution)/shard_map/pallas_call | solution.py:356
  76.3 2.1 %copy.7 = f32[2,8,12810]{2,1,0:T(8,128)} copy(f32[2,8,12810]{2,1,0:T(8,128)} %shard_map.46) | data formatting | bytes 1639680
Async XLA Ops:
  3.8 1.5 %copy-start = (s32[1280]{0:T(1024)S(1)}, s32[1280]{0:T(1024)}, u32[]{:S(2)}) copy-start(s32[1280]{0:T(1024)} %owned_ref.1) | copy-start | bytes 15364

commit v2 on v1

--- a/solution.py
+++ b/solution.py
@@ -21,6 +21,7 @@
     lane_tile,
     sizes,
     x_ref,
+    points_ref,
     waves_ref,
     owned_ref,
     legendre_ref,
@@ -102,12 +103,15 @@
 
     for v in range(-(-wave_count // 128)):
         width = min(128, wave_count - 128 * v)
-        line = waves_ref[:, 128 * v : 128 * v + width]
+        line = waves_ref[128 * v : 128 * v + width].reshape(1, width)
         wave_cols[128 * v : 128 * v + width] = jnp.broadcast_to(line, (128, width)).T
 
     wave_cols[wave_count : wave_count + 8] = jnp.full((8, 128), -1, jnp.int32)
 
     lane = lax.broadcasted_iota(jnp.int32, (n_lat * 8, 128), 1)
+    points = points_ref[...].reshape(1, rows_each)
+    limit = jnp.minimum(lax.shift_right_logical(points, 1), wave_count)
+    limit = jnp.concatenate([limit] * kinds, axis=1)
 
     def reorder(number):
         first = 8 * number
@@ -124,6 +128,8 @@
         picked = lax.dot_general(
             chosen, x_ref[...], NT, preferred_element_type=jnp.float32
         )
+        wide = jnp.concatenate([wave] * (-(-columns // 128)), axis=1)[:, :columns]
+        picked = jnp.where(wide < limit, picked, 0.0)
         for o in range(n_lat):
             part = picked[8 * o : 8 * o + sizes[number]]
             send_bufs[number][o] = part.astype(jnp.bfloat16)
@@ -348,10 +354,7 @@
     tiles = -(-lat_depth // 128)
 
     sizes = tuple(min(8, owner_waves - t) for t in range(0, owner_waves, 8))
-    wave_limit = jnp.minimum(cycle_points // 2, wave_count)
-    keep_mask = jnp.arange(wave_count, dtype=jnp.int32)[None, :] < wave_limit[:, None]
-    kept = jnp.where(keep_mask[None, :, None, None, :], fourier, jnp.zeros((), fourier.dtype))
-    x = jnp.transpose(kept, (0, 2, 3, 1, 4)).reshape(columns, wave_count)
+    x = jnp.transpose(fourier, (0, 2, 3, 1, 4)).reshape(columns, wave_count)
     vmem = pl.BlockSpec(memory_space=pltpu.VMEM)
     return pl.pallas_call(
         functools.partial(exchange_kernel, n_lat, n_fld, lane_tile, sizes),
@@ -359,8 +362,9 @@
         in_specs=[
             vmem,
             vmem,
+            vmem,
             pl.BlockSpec(memory_space=pltpu.SMEM),
-            pl.BlockSpec(memory_space=pl.ANY),
+            pl.BlockSpec(memory_space=pltpu.HBM),
         ],
         out_specs=vmem,
         scratch_shapes=[
@@ -382,14 +386,14 @@
             pltpu.SemaphoreType.DMA((n_fld - 1, owner_waves // 2 + 1)),
         ],
         compiler_params=pltpu.CompilerParams(
-            collective_id=0, has_side_effects=True, vmem_limit_bytes=56 * 2**20
+            collective_id=0, has_side_effects=True, vmem_limit_bytes=48 * 2**20
         ),
         cost_estimate=pl.CostEstimate(
             flops=4 * columns * wave_count * wave_count,
             bytes_accessed=total * lat_depth * 2,
             transcendentals=0,
         ),
-    )(x, wave_order.reshape(1, wave_count), wave_order, legendre.T)
+    )(x, cycle_points, wave_order, wave_order, legendre.T)
 
 
 def solution(mesh):

time: 78.6 us -> 71.6 us (0.911)
  other arithmetic: 3.8 us -> 0 us
  Pallas kernels: 70.4 us -> 68.8 us
  local copies, waits for them, and re-layouts: 4.16 us -> 2.64 us
    transpose x1 -> x0, other arithmetic: 3.03 us -> none  [shards(): x = jnp.transpose(kept, (0, 2, 3, 1, 4)).reshape(columns, wave_count)]
    pallas_call x1, Pallas kernels: 70.4 us -> 68.8 us  [shards(): pl.pallas_call(functools.partial(exchange_kernel, n_lat, n_fld, lane_tile...]
    unnamed x3 -> x5, local copies, waits for them, and re-layouts: 2.1 us -> 0.9 us
where the time goes in v2:
time: 71.6 us; the launch traced here: 71.5 us
  Pallas kernels  68.8 us (96%)
  local copies, waits for them, and re-layouts  2.64 us (4%)
    pallas_call x1, Pallas kernels, shards(): pl.pallas_call(functools.partial(exchange_kernel, n_lat, n_fld, lane_tile...  68.8 us
    transpose x1, local copies, waits for them, and re-layouts, shards(): x = jnp.transpose(fourier, (0, 2, 3, 1, 4)).reshape(columns, wave_count)  1.74 us

profile of v2, /device:TPU:1, one launch (start us, length us, event | category | flops | bytes accessed | tf_op | source)
XLA Modules:
  0.0 71.5 jit_solution(8650709702225788106)
XLA Ops:
  0.0 0.0 copy-start
  0.0 0.0 copy-start.1
  0.0 1.7 %copy.5 = bf16[2,4,2,40,1280]{4,3,2,1,0:T(8,128)(2,1)S(1)} copy(bf16[2,4,2,40,1280]{4,2,1,3,0:T(2,128)(2,1)} %bitcast.4) | data formatting | bytes 3276800 | tf_op jit(solution)/shard_map/transpose | solution.py:357
  1.7 0.0 copy-done
  1.8 0.0 copy-done.1
  1.8 68.8 %shard_map.46 = f32[2,8,12810]{2,1,0:T(8,128)S(1)} custom-call(bf16[640,1280]{1,0:T(8,128)(2,1)S(1)} %bitcast.3, s32[40]{0:T(128)S(1)} %copy-done.1, s32[1280]{0:T(1024)S(1)} %copy-done, s32[1280]{0:T(1024)S(1)} %copy-done, bf16[320,12810]{1,0:T(8,128)(2,1)} %bitcast.5), custom_call_target="tpu_custom_call" | custom-call | flops 4194304000 | bytes 8198400 | tf_op jit(solution)/shard_map/pallas_call | solution.py:359
  70.6 0.9 %copy.7 = f32[2,8,12810]{2,1,0:T(8,128)} copy(f32[2,8,12810]{2,1,0:T(8,128)S(1)} %shard_map.46) | data formatting | bytes 1639680
Async XLA Ops:
  0.0 1.7 %copy-start = (s32[1280]{0:T(1024)S(1)}, s32[1280]{0:T(1024)}, u32[]{:S(2)}) copy-start(s32[1280]{0:T(1024)} %owned_ref.1) | copy-start | bytes 15364
  0.0 1.8 %copy-start.1 = (s32[40]{0:T(128)S(1)}, s32[40]{0:T(128)}, u32[]{:S(2)}) copy-start(s32[40]{0:T(128)} %points_ref.1) | copy-start | bytes 484

commit v3 on v2

--- a/solution.py
+++ b/solution.py
@@ -91,12 +91,12 @@
 
     slot = fld * sources + hemi * depth + place
 
-    def copy_to(number, owner):
+    def copy_to(number, batch, owner):
         return pltpu.make_async_remote_copy(
             src_ref=send_bufs[number].at[owner],
             dst_ref=recv_bufs[number].at[slot],
-            send_sem=send_sem.at[number, owner],
-            recv_sem=recv_sem.at[number, slot],
+            send_sem=send_sem.at[number, batch],
+            recv_sem=recv_sem.at[number, fld],
             device_id=(owner, block),
             device_id_type=MESH,
         )
@@ -134,54 +134,71 @@
             part = picked[8 * o : 8 * o + sizes[number]]
             send_bufs[number][o] = part.astype(jnp.bfloat16)
 
-    def send(number):
-        def several(u, carry):
+    batches = n_lat // 8
+    own_batch, own_step = (5, 7) if n_lat == 64 else (0, 0)
+
+    def target(batch, n):
+        if n_lat != 64:
+            return (lat + batch * 8 + n) % n_lat
+        x = (lat // 16 + batch % 4 + n) % 4
+        z = (lat // 2 % 8 + (4, 1, 7, 2, 6, 3, 5, 0)[n]) % 8
+        return x * 16 + z * 2 + (lat + batch // 4 + n) % 2
+
+    def left(number, batch):
+        buf = send_bufs[number]
+        less = jnp.logical_and(own, batch == own_batch)
+
+        @pl.when(less)
+        def _():
+            done = buf.at[pl.ds(0, 7)]
+            pltpu.make_async_copy(done, done, send_sem.at[number, batch]).wait()
+
+        @pl.when(jnp.logical_not(less))
+        def _():
+            done = buf.at[pl.ds(0, 8)]
+            pltpu.make_async_copy(done, done, send_sem.at[number, batch]).wait()
+
+    def send(number, after=None):
+        def several(batch, carry):
+            if after is not None:
+                left(after, batch)
             for n in range(8):
-                if n_lat == 64:
-                    owner = (
-                        (lat // 16 + u % 4 + n) % 4 * 16
-                        + (lat // 2 % 8 + (4, 1, 7, 2, 6, 3, 5, 0)[n]) % 8 * 2
-                        + (lat + u // 4 + n) % 2
-                    )
-                else:
-                    owner = (lat + u * 8 + n) % n_lat
-                itself = jnp.logical_and(own, owner == lat)
+                owner = target(batch, n)
+                if n != own_step:
+                    copy_to(number, batch, owner).start()
+                    continue
+                itself = jnp.logical_and(own, batch == own_batch)
 
                 @pl.when(itself)
                 def _():
                     pltpu.make_async_copy(
                         send_bufs[number].at[owner],
                         recv_bufs[number].at[slot],
-                        recv_sem.at[number, slot],
+                        recv_sem.at[number, fld],
                     ).start()
 
                 @pl.when(jnp.logical_not(itself))
                 def _():
-                    copy_to(number, owner).start()
+                    copy_to(number, batch, owner).start()
 
             return carry
 
-        lax.fori_loop(0, n_lat // 8, several, 0)
+        lax.fori_loop(0, batches, several, 0)
 
     for number in range(n_groups):
         reorder(number)
         if number == 0:
             pl.semaphore_wait(barrier, n_lat + n_fld - 1 - own.astype(jnp.int32))
-        send(number)
+            send(number)
+    send(1, 0)
 
     def gather_group(number):
         count = sizes[number]
         recv_buf = recv_bufs[number]
 
         def gather_field(f, carry):
-            def arrived(s, carry):
-                at = f * sources + s
-                pltpu.make_async_copy(
-                    recv_buf.at[at], recv_buf.at[at], recv_sem.at[number, at]
-                ).wait()
-                return carry
-
-            lax.fori_loop(0, sources, arrived, 0)
+            here = recv_buf.at[pl.ds(f * sources, sources)]
+            pltpu.make_async_copy(here, here, recv_sem.at[number, f]).wait()
             for a in range(depth):
                 north = recv_buf[f * sources + a].astype(jnp.float32)
                 south = recv_buf[f * sources + depth + a].astype(jnp.float32)
@@ -230,7 +247,7 @@
         return pltpu.make_async_remote_copy(
             src_ref=part_send.at[peer, :, pl.ds(lo, width)],
             dst_ref=part_recv.at[d - 1, :, pl.ds(lo, width)],
-            send_sem=part_send_sem.at[d - 1, number],
+            send_sem=part_send_sem.at[d - 1],
             recv_sem=part_recv_sem.at[d - 1, number],
             device_id=(lat, peer),
             device_id_type=MESH,
@@ -302,6 +319,8 @@
         gather_group(number)
         first = 4 * number
         lax.fori_loop(first, first + sizes[number] // 2, pair_chunk, 0)
+        if number + 2 < n_groups:
+            send(number + 2, number + 1)
         if number == n_groups - 2:
             finished = 4 * number
             lax.fori_loop(0, finished, finish_pair, 0)
@@ -315,29 +334,16 @@
     for d in range(1, n_fld):
         part_copy(d, tail_from, tail_wide, pairs).start()
 
+    def last_left(batch, carry):
+        left(n_groups - 1, batch)
+        return carry
+
+    lax.fori_loop(0, batches, last_left, 0)
     lax.fori_loop(finished, pairs, finish_pair, 0)
     finish(tail_from, tail_wide, tail, pairs)
-
-    for number in range(n_groups):
-
-        def sent(owner, carry):
-            @pl.when(jnp.logical_not(jnp.logical_and(own, owner == lat)))
-            def _():
-                copy_to(number, owner).wait_send()
-
-            return carry
-
-        lax.fori_loop(0, n_lat, sent, 0)
-
-    def part_sent(c, carry):
-        start = pl.multiple_of(c * wave_count, min(wave_count, 1280))
-        for d in range(1, n_fld):
-            part_copy(d, start, wave_count, c).wait_send()
-        return carry
-
-    lax.fori_loop(0, pairs, part_sent, 0)
     for d in range(1, n_fld):
-        part_copy(d, tail_from, tail_wide, pairs).wait_send()
+        whole = part_send.at[(fld + d) % n_fld]
+        pltpu.make_async_copy(whole, whole, part_send_sem.at[d - 1]).wait()
 
 
 def shards(fourier, legendre, cycle_points, wave_order, lane_tile=256):
@@ -379,10 +385,10 @@
             pltpu.VMEM((per_wave, padded), jnp.float32),
             pltpu.VMEM((n_fld, kinds, padded), jnp.bfloat16),
             pltpu.VMEM((n_fld - 1, kinds, padded), jnp.bfloat16),
-            pltpu.SemaphoreType.DMA((len(sizes), n_lat)),
-            pltpu.SemaphoreType.DMA((len(sizes), slots)),
+            pltpu.SemaphoreType.DMA((len(sizes), n_lat // 8)),
+            pltpu.SemaphoreType.DMA((len(sizes), n_fld)),
             pltpu.SemaphoreType.DMA,
-            pltpu.SemaphoreType.DMA((n_fld - 1, owner_waves // 2 + 1)),
+            pltpu.SemaphoreType.DMA((n_fld - 1,)),
             pltpu.SemaphoreType.DMA((n_fld - 1, owner_waves // 2 + 1)),
         ],
         compiler_params=pltpu.CompilerParams(

time: 71.6 us -> 66.3 us (0.926)
  Pallas kernels: 68.8 us -> 63.5 us
    pallas_call x1, Pallas kernels: 68.8 us -> 63.5 us  [shards(): pl.pallas_call(functools.partial(exchange_kernel, n_lat, n_fld, lane_tile...]
where the time goes in v3:
time: 66.3 us; the launch traced here: 66.2 us
  Pallas kernels  63.5 us (96%)
  local copies, waits for them, and re-layouts  2.64 us (4%)
    pallas_call x1, Pallas kernels, shards(): pl.pallas_call(functools.partial(exchange_kernel, n_lat, n_fld, lane_tile...  63.5 us
    transpose x1, local copies, waits for them, and re-layouts, shards(): x = jnp.transpose(fourier, (0, 2, 3, 1, 4)).reshape(columns, wave_count)  1.74 us

profile of v3, /device:TPU:1, one launch (start us, length us, event | category | flops | bytes accessed | tf_op | source)
XLA Modules:
  0.0 66.2 jit_solution(6459217310216381447)
XLA Ops:
  0.0 0.0 copy-start
  0.0 0.0 copy-start.1
  0.0 1.7 %copy.5 = bf16[2,4,2,40,1280]{4,3,2,1,0:T(8,128)(2,1)S(1)} copy(bf16[2,4,2,40,1280]{4,2,1,3,0:T(2,128)(2,1)} %bitcast.4) | data formatting | bytes 3276800 | tf_op jit(solution)/shard_map/transpose | solution.py:363
  1.7 0.0 copy-done
  1.8 0.0 copy-done.1
  1.8 63.5 %shard_map.46 = f32[2,8,12810]{2,1,0:T(8,128)S(1)} custom-call(bf16[640,1280]{1,0:T(8,128)(2,1)S(1)} %bitcast.3, s32[40]{0:T(128)S(1)} %copy-done.1, s32[1280]{0:T(1024)S(1)} %copy-done, s32[1280]{0:T(1024)S(1)} %copy-done, bf16[320,12810]{1,0:T(8,128)(2,1)} %bitcast.5), custom_call_target="tpu_custom_call" | custom-call | flops 4194304000 | bytes 8198400 | tf_op jit(solution)/shard_map/pallas_call | solution.py:365
  65.3 0.9 %copy.7 = f32[2,8,12810]{2,1,0:T(8,128)} copy(f32[2,8,12810]{2,1,0:T(8,128)S(1)} %shard_map.46) | data formatting | bytes 1639680
Async XLA Ops:
  0.0 1.7 %copy-start = (s32[1280]{0:T(1024)S(1)}, s32[1280]{0:T(1024)}, u32[]{:S(2)}) copy-start(s32[1280]{0:T(1024)} %owned_ref.1) | copy-start | bytes 15364
  0.0 1.8 %copy-start.1 = (s32[40]{0:T(128)S(1)}, s32[40]{0:T(128)}, u32[]{:S(2)}) copy-start(s32[40]{0:T(128)} %points_ref.1) | copy-start | bytes 484

commit v4 on v3

--- a/solution.py
+++ b/solution.py
@@ -9,6 +9,7 @@
 
 MESH = pl.DeviceIdType.MESH
 NT = (((1,), (1,)), ((), ()))
+GROUPS = (4, 4, 4, 4, 4)
 
 
 def round_up(value, step):
@@ -57,6 +58,7 @@
     place = lat % depth
     columns, wave_count = x_ref.shape
     owner_waves = sum(sizes)
+    firsts = [sum(sizes[:number]) for number in range(n_groups)]
     kinds = part_send.shape[1]
     rows_each = columns // kinds
     pairs = owner_waves // 2
@@ -114,7 +116,7 @@
     limit = jnp.concatenate([limit] * kinds, axis=1)
 
     def reorder(number):
-        first = 8 * number
+        first = firsts[number]
         wave = jnp.concatenate(
             [wave_cols[o * owner_waves + first : o * owner_waves + first + 8] for o in range(n_lat)],
             axis=0,
@@ -210,7 +212,7 @@
                     joined = jnp.concatenate(
                         [mixed[a, 0:count, lo : lo + rows_each] for a in range(depth)], axis=1
                     )
-                    start = 8 * number * n_fld * kinds + f * kinds + k
+                    start = firsts[number] * n_fld * kinds + f * kinds + k
                     for v in range(-(-lat_depth // 128)):
                         width = min(128, lat_depth - 128 * v)
                         rows[v, pl.ds(start, count, stride=n_fld * kinds), 0:width] = joined[
@@ -317,12 +319,12 @@
     finished = 0
     for number in range(n_groups):
         gather_group(number)
-        first = 4 * number
+        first = firsts[number] // 2
         lax.fori_loop(first, first + sizes[number] // 2, pair_chunk, 0)
         if number + 2 < n_groups:
             send(number + 2, number + 1)
         if number == n_groups - 2:
-            finished = 4 * number
+            finished = firsts[max(number - 1, 1)] // 2
             lax.fori_loop(0, finished, finish_pair, 0)
 
     piece = left_over(pairs - 1, tail_from, tail)
@@ -359,7 +361,7 @@
     padded = round_up(total, 128)
     tiles = -(-lat_depth // 128)
 
-    sizes = tuple(min(8, owner_waves - t) for t in range(0, owner_waves, 8))
+    sizes = GROUPS
     x = jnp.transpose(fourier, (0, 2, 3, 1, 4)).reshape(columns, wave_count)
     vmem = pl.BlockSpec(memory_space=pltpu.VMEM)
     return pl.pallas_call(

time: 66.3 us -> 64.9 us (0.979)
  Pallas kernels: 63.5 us -> 62.1 us
    pallas_call x1, Pallas kernels: 63.5 us -> 62.1 us  [shards(): pl.pallas_call(functools.partial(exchange_kernel, n_lat, n_fld, lane_tile...]
where the time goes in v4:
time: 64.9 us; the launch traced here: 64.8 us
  Pallas kernels  62.1 us (96%)
  local copies, waits for them, and re-layouts  2.64 us (4%)
    pallas_call x1, Pallas kernels, shards(): pl.pallas_call(functools.partial(exchange_kernel, n_lat, n_fld, lane_tile...  62.1 us
    transpose x1, local copies, waits for them, and re-layouts, shards(): x = jnp.transpose(fourier, (0, 2, 3, 1, 4)).reshape(columns, wave_count)  1.74 us

profile of v4, /device:TPU:1, one launch (start us, length us, event | category | flops | bytes accessed | tf_op | source)
XLA Modules:
  0.0 64.8 jit_solution(233399383966971369)
XLA Ops:
  0.0 0.0 copy-start
  0.0 0.0 copy-start.1
  0.0 1.7 %copy.5 = bf16[2,4,2,40,1280]{4,3,2,1,0:T(8,128)(2,1)S(1)} copy(bf16[2,4,2,40,1280]{4,2,1,3,0:T(2,128)(2,1)} %bitcast.4) | data formatting | bytes 3276800 | tf_op jit(solution)/shard_map/transpose | solution.py:365
  1.7 0.0 copy-done
  1.8 0.0 copy-done.1
  1.8 62.1 %shard_map.46 = f32[2,8,12810]{2,1,0:T(8,128)S(1)} custom-call(bf16[640,1280]{1,0:T(8,128)(2,1)S(1)} %bitcast.3, s32[40]{0:T(128)S(1)} %copy-done.1, s32[1280]{0:T(1024)S(1)} %copy-done, s32[1280]{0:T(1024)S(1)} %copy-done, bf16[320,12810]{1,0:T(8,128)(2,1)} %bitcast.5), custom_call_target="tpu_custom_call" | custom-call | flops 4194304000 | bytes 8198400 | tf_op jit(solution)/shard_map/pallas_call | solution.py:367
  63.9 0.9 %copy.7 = f32[2,8,12810]{2,1,0:T(8,128)} copy(f32[2,8,12810]{2,1,0:T(8,128)S(1)} %shard_map.46) | data formatting | bytes 1639680
Async XLA Ops:
  0.0 1.7 %copy-start = (s32[1280]{0:T(1024)S(1)}, s32[1280]{0:T(1024)}, u32[]{:S(2)}) copy-start(s32[1280]{0:T(1024)} %owned_ref.1) | copy-start | bytes 15364
  0.0 1.8 %copy-start.1 = (s32[40]{0:T(128)S(1)}, s32[40]{0:T(128)}, u32[]{:S(2)}) copy-start(s32[40]{0:T(128)} %points_ref.1) | copy-start | bytes 484

commit v5 on v4

--- a/solution.py
+++ b/solution.py
@@ -198,29 +198,37 @@
         count = sizes[number]
         recv_buf = recv_bufs[number]
 
-        def gather_field(f, carry):
-            here = recv_buf.at[pl.ds(f * sources, sources)]
-            pltpu.make_async_copy(here, here, recv_sem.at[number, f]).wait()
-            for a in range(depth):
-                north = recv_buf[f * sources + a].astype(jnp.float32)
-                south = recv_buf[f * sources + depth + a].astype(jnp.float32)
-                mixed_sym[a, 0:count] = north + south
-                mixed_anti[a, 0:count] = north - south
+        side = 8 // count
+
+        def gather_fields(step, carry):
+            for j in range(side):
+                f = step * side + j
+                here = recv_buf.at[pl.ds(f * sources, sources)]
+                pltpu.make_async_copy(here, here, recv_sem.at[number, f]).wait()
+                lo = j * count
+                for a in range(depth):
+                    north = recv_buf[f * sources + a].astype(jnp.float32)
+                    south = recv_buf[f * sources + depth + a].astype(jnp.float32)
+                    mixed_sym[a, lo : lo + count] = north + south
+                    mixed_anti[a, lo : lo + count] = north - south
             for mixed, rows in ((mixed_sym, rows_sym), (mixed_anti, rows_anti)):
                 for k in range(kinds):
                     lo = k * rows_each
                     joined = jnp.concatenate(
-                        [mixed[a, 0:count, lo : lo + rows_each] for a in range(depth)], axis=1
+                        [mixed[a, 0 : side * count, lo : lo + rows_each] for a in range(depth)],
+                        axis=1,
                     )
-                    start = firsts[number] * n_fld * kinds + f * kinds + k
-                    for v in range(-(-lat_depth // 128)):
-                        width = min(128, lat_depth - 128 * v)
-                        rows[v, pl.ds(start, count, stride=n_fld * kinds), 0:width] = joined[
-                            :, 128 * v : 128 * v + width
-                        ]
+                    for j in range(side):
+                        start = firsts[number] * n_fld * kinds + (step * side + j) * kinds + k
+                        part = joined[j * count : (j + 1) * count]
+                        for v in range(-(-lat_depth // 128)):
+                            width = min(128, lat_depth - 128 * v)
+                            rows[v, pl.ds(start, count, stride=n_fld * kinds), 0:width] = part[
+                                :, 128 * v : 128 * v + width
+                            ]
             return carry
 
-        lax.fori_loop(0, n_fld, gather_field, 0)
+        lax.fori_loop(0, n_fld // side, gather_fields, 0)
 
     per_wave = n_fld * kinds
     even = wave_count // 2 + 1

time: 64.9 us -> 64.2 us (0.989)
  Pallas kernels: 62.1 us -> 61.4 us
    pallas_call x1, Pallas kernels: 62.1 us -> 61.4 us  [shards(): pl.pallas_call(functools.partial(exchange_kernel, n_lat, n_fld, lane_tile...]
where the time goes in v5:
time: 64.2 us; the launch traced here: 64.1 us
  Pallas kernels  61.4 us (96%)
  local copies, waits for them, and re-layouts  2.64 us (4%)
    pallas_call x1, Pallas kernels, shards(): pl.pallas_call(functools.partial(exchange_kernel, n_lat, n_fld, lane_tile...  61.4 us
    transpose x1, local copies, waits for them, and re-layouts, shards(): x = jnp.transpose(fourier, (0, 2, 3, 1, 4)).reshape(columns, wave_count)  1.74 us

profile of v5, /device:TPU:1, one launch (start us, length us, event | category | flops | bytes accessed | tf_op | source)
XLA Modules:
  0.0 64.1 jit_solution(3615258681655060568)
XLA Ops:
  0.0 0.0 copy-start
  0.0 0.0 copy-start.1
  0.0 1.7 %copy.5 = bf16[2,4,2,40,1280]{4,3,2,1,0:T(8,128)(2,1)S(1)} copy(bf16[2,4,2,40,1280]{4,2,1,3,0:T(2,128)(2,1)} %bitcast.4) | data formatting | bytes 3276800 | tf_op jit(solution)/shard_map/transpose | solution.py:373
  1.7 0.0 copy-done
  1.8 0.0 copy-done.1
  1.8 61.4 %shard_map.46 = f32[2,8,12810]{2,1,0:T(8,128)S(1)} custom-call(bf16[640,1280]{1,0:T(8,128)(2,1)S(1)} %bitcast.3, s32[40]{0:T(128)S(1)} %copy-done.1, s32[1280]{0:T(1024)S(1)} %copy-done, s32[1280]{0:T(1024)S(1)} %copy-done, bf16[320,12810]{1,0:T(8,128)(2,1)} %bitcast.5), custom_call_target="tpu_custom_call" | custom-call | flops 4194304000 | bytes 8198400 | tf_op jit(solution)/shard_map/pallas_call | solution.py:375
  63.2 0.9 %copy.7 = f32[2,8,12810]{2,1,0:T(8,128)} copy(f32[2,8,12810]{2,1,0:T(8,128)S(1)} %shard_map.46) | data formatting | bytes 1639680
Async XLA Ops:
  0.0 1.7 %copy-start = (s32[1280]{0:T(1024)S(1)}, s32[1280]{0:T(1024)}, u32[]{:S(2)}) copy-start(s32[1280]{0:T(1024)} %owned_ref.1) | copy-start | bytes 15364
  0.0 1.8 %copy-start.1 = (s32[40]{0:T(128)S(1)}, s32[40]{0:T(128)}, u32[]{:S(2)}) copy-start(s32[40]{0:T(128)} %points_ref.1) | copy-start | bytes 484

commit v6 on v5

--- a/solution.py
+++ b/solution.py
@@ -110,15 +110,18 @@
 
     wave_cols[wave_count : wave_count + 8] = jnp.full((8, 128), -1, jnp.int32)
 
-    lane = lax.broadcasted_iota(jnp.int32, (n_lat * 8, 128), 1)
     points = points_ref[...].reshape(1, rows_each)
     limit = jnp.minimum(lax.shift_right_logical(points, 1), wave_count)
     limit = jnp.concatenate([limit] * kinds, axis=1)
 
     def reorder(number):
-        first = firsts[number]
+        first, count = firsts[number], sizes[number]
+        lane = lax.broadcasted_iota(jnp.int32, (n_lat * count, 128), 1)
         wave = jnp.concatenate(
-            [wave_cols[o * owner_waves + first : o * owner_waves + first + 8] for o in range(n_lat)],
+            [
+                wave_cols[o * owner_waves + first : o * owner_waves + first + count]
+                for o in range(n_lat)
+            ],
             axis=0,
         )
         pieces = []
@@ -133,7 +136,7 @@
         wide = jnp.concatenate([wave] * (-(-columns // 128)), axis=1)[:, :columns]
         picked = jnp.where(wide < limit, picked, 0.0)
         for o in range(n_lat):
-            part = picked[8 * o : 8 * o + sizes[number]]
+            part = picked[count * o : count * (o + 1)]
             send_bufs[number][o] = part.astype(jnp.bfloat16)
 
     batches = n_lat // 8
@@ -324,9 +327,21 @@
         return carry
 
     load.wait()
+    def send_tail():
+        piece = left_over(pairs - 1, tail_from, tail)
+        partial[:, tail_from : tail_from + tail] = piece
+        for f in range(n_fld):
+            part_send[f, :, tail_from : tail_from + tail] = piece[
+                f * kinds : (f + 1) * kinds
+            ].astype(jnp.bfloat16)
+        for d in range(1, n_fld):
+            part_copy(d, tail_from, tail_wide, pairs).start()
+
     finished = 0
     for number in range(n_groups):
         gather_group(number)
+        if number == n_groups - 1:
+            send_tail()
         first = firsts[number] // 2
         lax.fori_loop(first, first + sizes[number] // 2, pair_chunk, 0)
         if number + 2 < n_groups:
@@ -334,15 +349,6 @@
         if number == n_groups - 2:
             finished = firsts[max(number - 1, 1)] // 2
             lax.fori_loop(0, finished, finish_pair, 0)
-
-    piece = left_over(pairs - 1, tail_from, tail)
-    partial[:, tail_from : tail_from + tail] = piece
-    for f in range(n_fld):
-        part_send[f, :, tail_from : tail_from + tail] = piece[
-            f * kinds : (f + 1) * kinds
-        ].astype(jnp.bfloat16)
-    for d in range(1, n_fld):
-        part_copy(d, tail_from, tail_wide, pairs).start()
 
     def last_left(batch, carry):
         left(n_groups - 1, batch)

time: 64.2 us -> 64.4 us (level)
  no operation moved by 1% of the time
where the time goes in v6:
time: 64.4 us; the launch traced here: 64.3 us
  Pallas kernels  61.7 us (96%)
  local copies, waits for them, and re-layouts  2.64 us (4%)
    pallas_call x1, Pallas kernels, shards(): pl.pallas_call(functools.partial(exchange_kernel, n_lat, n_fld, lane_tile...  61.7 us
    transpose x1, local copies, waits for them, and re-layouts, shards(): x = jnp.transpose(fourier, (0, 2, 3, 1, 4)).reshape(columns, wave_count)  1.74 us

profile of v6, /device:TPU:1, one launch (start us, length us, event | category | flops | bytes accessed | tf_op | source)
XLA Modules:
  0.0 64.3 jit_solution(6156161191065328217)
XLA Ops:
  0.0 0.0 copy-start
  0.0 0.0 copy-start.1
  0.0 1.7 %copy.5 = bf16[2,4,2,40,1280]{4,3,2,1,0:T(8,128)(2,1)S(1)} copy(bf16[2,4,2,40,1280]{4,2,1,3,0:T(2,128)(2,1)} %bitcast.4) | data formatting | bytes 3276800 | tf_op jit(solution)/shard_map/transpose | solution.py:379
  1.7 0.0 copy-done
  1.8 0.0 copy-done.1
  1.8 61.7 %shard_map.46 = f32[2,8,12810]{2,1,0:T(8,128)S(1)} custom-call(bf16[640,1280]{1,0:T(8,128)(2,1)S(1)} %bitcast.3, s32[40]{0:T(128)S(1)} %copy-done.1, s32[1280]{0:T(1024)S(1)} %copy-done, s32[1280]{0:T(1024)S(1)} %copy-done, bf16[320,12810]{1,0:T(8,128)(2,1)} %bitcast.5), custom_call_target="tpu_custom_call" | custom-call | flops 4194304000 | bytes 8198400 | tf_op jit(solution)/shard_map/pallas_call | solution.py:381
  63.4 0.9 %copy.7 = f32[2,8,12810]{2,1,0:T(8,128)} copy(f32[2,8,12810]{2,1,0:T(8,128)S(1)} %shard_map.46) | data formatting | bytes 1639680
Async XLA Ops:
  0.0 1.7 %copy-start = (s32[1280]{0:T(1024)S(1)}, s32[1280]{0:T(1024)}, u32[]{:S(2)}) copy-start(s32[1280]{0:T(1024)} %owned_ref.1) | copy-start | bytes 15364
  0.0 1.8 %copy-start.1 = (s32[40]{0:T(128)S(1)}, s32[40]{0:T(128)}, u32[]{:S(2)}) copy-start(s32[40]{0:T(128)} %points_ref.1) | copy-start | bytes 484
